TPU v7x, 512 devices: a whole 4x4x16 slice. The times are simulated.
512 devices in a mesh: leaf: 32 (over x, y, core), front: 16 (over z).
Axes of the slice: x: 4, y: 4, z: 16, core: 2. Of those that a mesh axis runs over, the one named last changes fastest.
Arguments:
- panel_0: float32 [2, 1024, 1024], P(None, 'front', 'leaf'), as said below
- panel_1: float32 [2, 1024, 2048], P(None, 'front', 'leaf'), as said below
- panel_2: float32 [2, 1024, 4096], P(None, 'front', 'leaf'), as said below
- panel_3: float32 [2, 1024, 8192], P(None, 'front', 'leaf'), as said below
- load_0: float32 [1024, 128], P('leaf'), may hold values from -6 to 6
- load_1: float32 [2048, 128], P('leaf'), may hold values from -6 to 6
- load_2: float32 [4096, 128], P('leaf'), may hold values from -6 to 6
- load_3: float32 [8192, 128], P('leaf'), may hold values from -6 to 6
- inflow: float32 [8, 1024, 128], P(None, 'front'), may hold values from -6 to 6
- above_solution: float32 [1024, 128], replicated, may hold values from -6 to 6
- block_maps: int32 [14, 16], replicated, may hold values from 0 to 31, as said below
Outputs:
- solution_0: float32 [1024, 128], P(('leaf', 'front'))
- solution_1: float32 [2048, 128], P(('leaf', 'front'))
- solution_2: float32 [4096, 128], P(('leaf', 'front'))
- solution_3: float32 [8192, 128], P(('leaf', 'front'))
- top_update: float32 [1024, 128], P('front')
Inputs may be any that keep to these rules, and one draw needn't show every extreme that they name: `block_maps`: the 16 entries of each row are distinct. `panel_0`: within each front the pivot block K is lower triangular with diagonal entries of 0.8 to 1.25. `panel_1`: within each front the pivot block K is lower triangular with diagonal entries of 0.8 to 1.25. `panel_2`: within each front the pivot block K is lower triangular with diagonal entries of 0.8 to 1.25. `panel_3`: within each front the pivot block K is lower triangular with diagonal entries of 0.8 to 1.25.
All inputs are finite; a program needn't handle non-finite values.
Results may differ from a plain program's by a relative error of at most 0.00013.
Values sent between devices are 32-bit elements; how exact they have to be, the bound alone decides.
No kernel may reach another device: no remote copies, remote signals or barrier semaphores. Data moves between devices by JAX's collectives and lax.ppermute only.
A program may use at most 64 MiB of HBM per device.

v0:
```python
import jax
import jax.numpy as jnp
from jax import lax
from jax.sharding import PartitionSpec as P

exact_precision = lax.Precision.HIGHEST


def partner_2(value, axis, distance):
    mask = 2**distance
    pairs = [(source, source ^ mask) for source in range(lax.axis_size(axis))]
    return lax.ppermute(value, axis, pairs)


def group_total(partial_sum, group_bits, level_id):
    leaf_pos = lax.axis_index("leaf")
    group_count = 1 << level_id
    slot_id = leaf_pos >> group_bits
    chosen = (jnp.arange(group_count, dtype=jnp.int32) == slot_id).astype(jnp.float32)
    spread_out = chosen.reshape((group_count,) + (1,) * partial_sum.ndim) * partial_sum[None]
    totals = lax.psum(spread_out, "leaf")
    return lax.dynamic_index_in_dim(totals, slot_id, 0, keepdims=False)


def group_concat(column_block, group_bits):
    leaf_pos = lax.axis_index("leaf")
    for section_bit in range(group_bits):
        partner = partner_2(column_block, "leaf", section_bit)
        upper_half = leaf_pos >> section_bit & 1 == 1
        column_block = jnp.where(
            upper_half,
            jnp.concatenate([partner, column_block], 0),
            jnp.concatenate([column_block, partner], 0),
        )
    return column_block


def place_blocks(map_row, values, block_rows):
    block_count = map_row.shape[0]
    targets = jnp.arange(2 * block_count, dtype=jnp.int32)
    selector_matrix = (targets[:, None] == map_row[None, :]).astype(jnp.float32)
    factor_blocks = values.reshape(block_count, block_rows, values.shape[1])
    return jnp.einsum("du,uye->dye", selector_matrix, factor_blocks, precision=exact_precision)


def lift_update(update_block, level_id, group_bits, block_maps, sep_rows):
    leaf_pos = lax.axis_index("leaf")
    front_pos = lax.axis_index("front")
    block_rows = update_block.shape[0]
    block_count = sep_rows // block_rows
    group_size = 1 << group_bits
    child_id = leaf_pos >> group_bits
    base_row = (1 << level_id) - 2
    own_map = lax.dynamic_index_in_dim(block_maps, base_row + child_id, 0, keepdims=False)
    parent_pos = leaf_pos % (2 * group_size)
    parent_rows = sep_rows // (2 * group_size)
    other_map = lax.dynamic_index_in_dim(block_maps, base_row + (child_id ^ 1), 0, keepdims=False)
    partner_block = partner_2(update_block, "leaf", group_bits)
    own_full, other_full = (
        lax.all_gather(update_block, "front", axis=0, tiled=True),
        lax.all_gather(partner_block, "front", axis=0, tiled=True),
    )
    placed = place_blocks(own_map, own_full, block_rows) + place_blocks(
        other_map, other_full, block_rows
    )
    separator = placed[:block_count].reshape(sep_rows, -1)
    sep_part = lax.dynamic_slice_in_dim(separator, parent_pos * parent_rows, parent_rows, 0)
    border = lax.dynamic_index_in_dim(placed, block_count + front_pos, 0, keepdims=False)
    return (sep_part, border)


def on_device(
    panel_0,
    panel_1,
    panel_2,
    panel_3,
    load_0,
    load_1,
    load_2,
    load_3,
    inflow,
    above_solution,
    block_maps,
):
    panels = (panel_0, panel_1, panel_2, panel_3)
    load_list = (load_0, load_1, load_2, load_3)
    level_count = len(panels)
    leaf_pos = lax.axis_index("leaf")
    front_pos = lax.axis_index("front")
    front_count = lax.axis_size("front")
    total_bits = lax.axis_size("leaf").bit_length() - 1
    block_rows = panel_0.shape[1]
    sep_rows = block_rows * front_count
    solved = [None] * level_count
    lifted = None
    top_block = None
    for level_id in range(level_count - 1, -1, -1):
        group_bits = total_bits - level_id
        right_side = load_list[level_id]
        if level_id == level_count - 1:
            front_id = leaf_pos >> group_bits
            border = lax.dynamic_index_in_dim(inflow, front_id, 0, keepdims=False)
        else:
            right_side = right_side + lifted[0]
            border = lifted[1]
        partial_sum = jnp.einsum(
            "ksc,cr->ksr", panels[level_id], right_side, precision=exact_precision
        )
        totals = group_total(partial_sum, group_bits, level_id)
        solved[level_id] = totals[0]
        update_block = border - totals[1]
        if level_id > 0:
            lifted = lift_update(update_block, level_id, group_bits, block_maps, sep_rows)
        else:
            top_block = update_block
    upper_full = above_solution
    upper_block = lax.dynamic_slice_in_dim(above_solution, front_pos * block_rows, block_rows, 0)
    targets = jnp.arange(2 * front_count, dtype=jnp.int32)
    pieces = []
    for level_id in range(level_count):
        group_bits = total_bits - level_id
        stacked = jnp.stack([solved[level_id], -upper_block])
        partial_sum = jnp.einsum(
            "ksc,ksr->cr", panels[level_id], stacked, precision=exact_precision
        )
        column_block = lax.psum(partial_sum, "front")
        span_rows = column_block.shape[0] // front_count
        pieces.append(lax.dynamic_slice_in_dim(column_block, front_pos * span_rows, span_rows, 0))
        if level_id < level_count - 1:
            full_solution = group_concat(column_block, group_bits)
            ancestor_blocks = jnp.concatenate([full_solution, upper_full], 0).reshape(
                2 * front_count, block_rows, -1
            )
            child_id = leaf_pos >> group_bits - 1
            child_map = lax.dynamic_index_in_dim(
                block_maps, (2 << level_id) - 2 + child_id, 0, keepdims=False
            )
            selector_matrix = (child_map[:, None] == targets[None, :]).astype(jnp.float32)
            upper_factor_blocks = jnp.einsum(
                "gq,qzk->gzk", selector_matrix, ancestor_blocks, precision=exact_precision
            )
            upper_full = upper_factor_blocks.reshape(sep_rows, -1)
            upper_block = lax.dynamic_index_in_dim(
                upper_factor_blocks, front_pos, 0, keepdims=False
            )
    return (pieces[0], pieces[1], pieces[2], pieces[3], top_block)


def solution(mesh):
    in_specs = (
        P(None, "front", "leaf"),
        P(None, "front", "leaf"),
        P(None, "front", "leaf"),
        P(None, "front", "leaf"),
        P("leaf", None),
        P("leaf", None),
        P("leaf", None),
        P("leaf", None),
        P(None, "front", None),
        P(),
        P(),
    )
    out_specs = (
        P(("leaf", "front"), None),
        P(("leaf", "front"), None),
        P(("leaf", "front"), None),
        P(("leaf", "front"), None),
        P("front", None),
    )
    return jax.shard_map(
        on_device, mesh=mesh, in_specs=in_specs, out_specs=out_specs, check_vma=False
    )
```

profile of v0, /device:TPU:2, one launch (start us, length us, event | category | flops | bytes accessed | tf_op | source)
XLA Modules:
  0.0 1208.8 jit_solution(1407500976551751530)
XLA Ops:
  11.1 138.3 %all-reduce.7.cloned.1.call-done = f32[8,2,64,128]{3,2,1,0:T(8,128)} async-done(((f32[8,2,64,128]{3,2,1,0:T(8,128)}), f32[8,2,64,128]{3,2,1,0:T(8,128)}) %all-reduce.7.cloned.1.call-update) | async-done | bytes 524304 | tf_op jit(solution)/shard_map/psum | solution.py:21
  150.2 4.2 collective-permute-start
  154.4 33.1 %all_gather.18 = f32[1024,128]{1,0:T(8,128)S(1)} all-gather(f32[64,128]{1,0:T(8,128)S(1)} %fusion.32), channel_id=1, replica_groups=mesh['leaf'=32,'front'=16] {'front'}, dimensions={0}, use_global_device_ids=true | all-gather | bytes 557056 | tf_op jit(solution)/shard_map/all_gather | solution.py:60
  188.5 30.6 %all_gather.19 = f32[1024,128]{1,0:T(8,128)S(1)} all-gather(f32[64,128]{1,0:T(8,128)S(1)} %collective-permute-done), channel_id=1, replica_groups=mesh['leaf'=32,'front'=16] {'front'}, dimensions={0}, use_global_device_ids=true | all-gather | bytes 557056 | tf_op jit(solution)/shard_map/all_gather | solution.py:61
  222.2 127.9 %all-reduce.9.cloned.1.call-done = f32[4,2,64,128]{3,2,1,0:T(8,128)} async-done(((f32[4,2,64,128]{3,2,1,0:T(8,128)}), f32[4,2,64,128]{3,2,1,0:T(8,128)}) %all-reduce.9.cloned.1.call-update) | async-done | bytes 262160 | tf_op jit(solution)/shard_map/psum | solution.py:21
  353.8 33.6 %all_gather.20 = f32[1024,128]{1,0:T(8,128)S(1)} all-gather(f32[64,128]{1,0:T(8,128)S(1)} %fusion.31), channel_id=1, replica_groups=mesh['leaf'=32,'front'=16] {'front'}, dimensions={0}, use_global_device_ids=true | all-gather | bytes 557056 | tf_op jit(solution)/shard_map/all_gather | solution.py:60
  388.3 30.1 %all_gather.21 = f32[1024,128]{1,0:T(8,128)S(1)} all-gather(f32[64,128]{1,0:T(8,128)S(1)} %collective-permute-done.1), channel_id=1, replica_groups=mesh['leaf'=32,'front'=16] {'front'}, dimensions={0}, use_global_device_ids=true | all-gather | bytes 557056 | tf_op jit(solution)/shard_map/all_gather | solution.py:61
  421.3 126.1 %all-reduce.11.cloned.1.call-done = f32[2,2,64,128]{3,2,1,0:T(8,128)} async-done(((f32[2,2,64,128]{3,2,1,0:T(8,128)}), f32[2,2,64,128]{3,2,1,0:T(8,128)}) %all-reduce.11.cloned.1.call-update) | async-done | bytes 131088 | tf_op jit(solution)/shard_map/psum | solution.py:21
  548.2 5.2 collective-permute-start.2
  553.4 33.3 %all_gather.22 = f32[1024,128]{1,0:T(8,128)S(1)} all-gather(f32[64,128]{1,0:T(8,128)S(1)} %fusion.30), channel_id=1, replica_groups=mesh['leaf'=32,'front'=16] {'front'}, dimensions={0}, use_global_device_ids=true | all-gather | bytes 557056 | tf_op jit(solution)/shard_map/all_gather | solution.py:60
  587.6 30.3 %all_gather.23 = f32[1024,128]{1,0:T(8,128)S(1)} all-gather(f32[64,128]{1,0:T(8,128)S(1)} %collective-permute-done.2), channel_id=1, replica_groups=mesh['leaf'=32,'front'=16] {'front'}, dimensions={0}, use_global_device_ids=true | all-gather | bytes 557056 | tf_op jit(solution)/shard_map/all_gather | solution.py:61
  620.7 120.9 %all-reduce.13.cloned.1.call-done = f32[1,2,64,128]{3,2,1,0:T(8,128)} async-done(((f32[1,2,64,128]{3,2,1,0:T(8,128)}), f32[1,2,64,128]{3,2,1,0:T(8,128)}) %all-reduce.13.cloned.1.call-update) | async-done | bytes 65552 | tf_op jit(solution)/shard_map/psum | solution.py:21
  742.6 56.8 %psum.60 = f32[32,128]{1,0:T(8,128)S(1)} all-reduce(f32[32,128]{1,0:T(8,128)S(1)} %convolution_bitcast_fusion.5), channel_id=1, replica_groups=mesh['leaf'=32,'front'=16] {'front'}, use_global_device_ids=true, to_apply=%region_4.5 | all-reduce | flops 4096 | bytes 32768 | tf_op jit(solution)/shard_map/psum | solution.py:126
  808.2 4.6 collective-permute-start.5
  822.8 4.1 collective-permute-start.7
  827.6 4.9 collective-permute-done.7
  834.2 53.5 %psum.61 = f32[64,128]{1,0:T(8,128)S(1)} all-reduce(f32[64,128]{1,0:T(8,128)S(1)} %convolution_bitcast_fusion.4), channel_id=1, replica_groups=mesh['leaf'=32,'front'=16] {'front'}, use_global_device_ids=true, to_apply=%region_5.6 | all-reduce | flops 8192 | bytes 65536 | tf_op jit(solution)/shard_map/psum | solution.py:126
  896.9 4.6 collective-permute-start.10
  901.5 3.8 collective-permute-done.10
  909.8 3.8 collective-permute-done.11
  915.9 129.0 %all-reduce.15.cloned.1.call-done = f32[128,128]{0,1:T(8,128)} async-done(((f32[128,128]{0,1:T(8,128)}), f32[128,128]{0,1:T(8,128)}) %all-reduce.15.cloned.1.call-update) | async-done | bytes 65552 | tf_op jit(solution)/shard_map/psum | solution.py:126
  1056.6 4.9 collective-permute-start.14
  1063.1 4.4 collective-permute-done.14
  1071.7 128.7 %all-reduce.17.cloned.1.call-done = f32[256,128]{0,1:T(8,128)} async-done(((f32[256,128]{0,1:T(8,128)}), f32[256,128]{0,1:T(8,128)}) %all-reduce.17.cloned.1.call-update) | async-done | bytes 131088 | tf_op jit(solution)/shard_map/psum | solution.py:126
  (125 shorter events, 77.6 us)
Async XLA Ops:
  7.2 0.9 copy-start
  7.2 142.3 %all-reduce.7.cloned.1.call-start = ((), (), s32[]{:S(2)}) async-start(), calls=%async_computation | async-start | bytes 1048576 | tf_op jit(solution)/shard_map/psum | solution.py:21
  10.2 339.9 %all-reduce.9.cloned.1.call-start = ((), (), s32[]{:S(2)}) async-start(), calls=%async_computation.1 | async-start | bytes 524288 | tf_op jit(solution)/shard_map/psum | solution.py:21
  150.2 38.2 %collective-permute-start = (f32[64,128]{1,0:T(8,128)S(1)}, f32[64,128]{1,0:T(8,128)S(1)}, u32[]{:S(2)}, u32[]{:S(2)}) collective-permute-start(f32[64,128]{1,0:T(8,128)S(1)} %fusion.32), channel_id=1, source_target_pairs={{0,64},{16,80},{32,96},{48,112},{64,0},{80,16},{96,32},{112,48},{1... | collective-permute-start | bytes 98312 | tf_op jit(solution)/shard_map/ppermute | solution.py:12
  222.0 325.4 %all-reduce.11.cloned.1.call-start = ((), (), s32[]{:S(2)}) async-start(), calls=%async_computation.2 | async-start | bytes 262144 | tf_op jit(solution)/shard_map/psum | solution.py:21
  350.8 37.5 %collective-permute-start.1 = (f32[64,128]{1,0:T(8,128)S(1)}, f32[64,128]{1,0:T(8,128)S(1)}, u32[]{:S(2)}, u32[]{:S(2)}) collective-permute-start(f32[64,128]{1,0:T(8,128)S(1)} %fusion.31), channel_id=1, source_target_pairs={{0,128},{16,144},{32,160},{48,176},{64,192},{80,208},{96,224},{112... | collective-permute-start | bytes 98312 | tf_op jit(solution)/shard_map/ppermute | solution.py:12
  421.2 320.4 %all-reduce.13.cloned.1.call-start = ((), (), s32[]{:S(2)}) async-start(), calls=%async_computation.3 | async-start | bytes 131072 | tf_op jit(solution)/shard_map/psum | solution.py:21
  548.2 39.5 %collective-permute-start.2 = (f32[64,128]{1,0:T(8,128)S(1)}, f32[64,128]{1,0:T(8,128)S(1)}, u32[]{:S(2)}, u32[]{:S(2)}) collective-permute-start(f32[64,128]{1,0:T(8,128)S(1)} %fusion.30), channel_id=1, source_target_pairs={{0,256},{16,272},{32,288},{48,304},{64,320},{80,336},{96,352},{112... | collective-permute-start | bytes 98312 | tf_op jit(solution)/shard_map/ppermute | solution.py:12
  619.0 1.7 copy-start.1
  620.7 424.2 %all-reduce.15.cloned.1.call-start = ((), (), s32[]{:S(2)}) async-start(), calls=%async_computation.4 | async-start | bytes 131072 | tf_op jit(solution)/shard_map/psum | solution.py:126
  799.4 3.1 collective-permute-start.3
  802.4 5.8 collective-permute-start.4
  808.2 7.7 collective-permute-start.5
  815.9 6.9 collective-permute-start.6
  822.8 9.8 collective-permute-start.7
  887.7 3.1 collective-permute-start.8
  890.8 6.2 collective-permute-start.9
  896.9 8.4 collective-permute-start.10
  905.3 8.3 collective-permute-start.11
  915.9 284.5 %all-reduce.17.cloned.1.call-start = ((), (), s32[]{:S(2)}) async-start(), calls=%async_computation.5 | async-start | bytes 262144 | tf_op jit(solution)/shard_map/psum | solution.py:126
  1044.9 3.3 collective-permute-start.12
  1049.1 7.5 collective-permute-start.13
  1053.4 8.8 copy-start.6
  1056.6 10.9 collective-permute-start.14
  (7 other events, 5.7 us)
Sparse Core Ops, SparseCore 0:
  11.2 138.1 all-reduce.6
  222.1 127.8 all-reduce.8
  421.4 126.0 all-reduce.10
  620.8 120.7 all-reduce.12
  916.0 128.8 all-reduce.14
  1070.3 130.0 all-reduce.16
where the time goes:
time: 1210 us
  waiting for transfers between devices  806 us (67%)
  blocking collectives  301 us (25%)
  starting transfers between devices  53.6 us (4%)
  between operations  14.8 us (1%)
  matrix products  13.7 us (1%)
    psum x4, waiting for transfers between devices, group_total(): totals = lax.psum(spread_out, 'leaf')  513 us
    psum x2, waiting for transfers between devices, on_device(): column_block = lax.psum(partial_sum, 'front')  258 us
    psum x2, blocking collectives, on_device(): column_block = lax.psum(partial_sum, 'front')  110 us
    all_gather x3, blocking collectives, lift_update(): lax.all_gather(update_block, 'front', axis=0, tiled=True)  100 us
    all_gather x3, blocking collectives, lift_update(): lax.all_gather(partner_block, 'front', axis=0, tiled=True)  91 us
    ppermute x15, starting transfers between devices, partner_2(): return lax.ppermute(value, axis, pairs)  53.4 us
    ppermute x15, waiting for transfers between devices, partner_2(): return lax.ppermute(value, axis, pairs)  35.6 us
  transfers between devices with their start and end apart: 21, of which 18 were waited for; matrix products, arithmetic and copies ran while one was open for 1% of the time, Pallas kernels for 0%

commit v1 on v0

--- a/solution.py
+++ b/solution.py
@@ -4,6 +4,11 @@
 from jax.sharding import PartitionSpec as P
 
 exact_precision = lax.Precision.HIGHEST
+
+
+def gather_and_add(value, mesh_axis):
+    shards = lax.all_gather(value, mesh_axis)
+    return jnp.sum(shards, axis=0)
 
 
 def partner_2(value, axis, distance):
@@ -18,7 +23,7 @@
     slot_id = leaf_pos >> group_bits
     chosen = (jnp.arange(group_count, dtype=jnp.int32) == slot_id).astype(jnp.float32)
     spread_out = chosen.reshape((group_count,) + (1,) * partial_sum.ndim) * partial_sum[None]
-    totals = lax.psum(spread_out, "leaf")
+    totals = gather_and_add(spread_out, "leaf")
     return lax.dynamic_index_in_dim(totals, slot_id, 0, keepdims=False)
 
 

time: 1210 us -> 982 us (0.81)
  waiting for transfers between devices: 806 us -> 579 us
  other arithmetic: 6.93 us -> 21.2 us
    psum x4 -> x0, waiting for transfers between devices: 513 us -> none  [group_total(): totals = lax.psum(spread_out, 'leaf')]
    all_gather x0 -> x4, waiting for transfers between devices: none -> 270 us  [gather_and_add(): shards = lax.all_gather(value, mesh_axis)]
    ppermute x15, waiting for transfers between devices: 35.6 us -> 51.8 us  [partner_2(): return lax.ppermute(value, axis, pairs)]
    reduce_sum x0 -> x4, other arithmetic: none -> 15.6 us  [gather_and_add(): return jnp.sum(shards, axis=0)]
  transfers between devices with their start and end apart: 21 -> 21, of which waited for: 18 -> 21; matrix products, arithmetic and copies ran while one was open for 1% -> 1% of each run, Pallas kernels for 0% -> 0%
where the time goes in v1:
time: 982 us; the launch traced here: 981 us
  waiting for transfers between devices  579 us (59%)
  blocking collectives  300 us (31%)
  starting transfers between devices  45 us (5%)
  other arithmetic  21.2 us (2%)
  between operations  14.8 us (2%)
  matrix products  13.7 us (1%)
    all_gather x4, waiting for transfers between devices, gather_and_add(): shards = lax.all_gather(value, mesh_axis)  270 us
    psum x2, waiting for transfers between devices, on_device(): column_block = lax.psum(partial_sum, 'front')  258 us
    psum x2, blocking collectives, on_device(): column_block = lax.psum(partial_sum, 'front')  110 us
    all_gather x3, blocking collectives, lift_update(): lax.all_gather(update_block, 'front', axis=0, tiled=True)  101 us
    all_gather x3, blocking collectives, lift_update(): lax.all_gather(partner_block, 'front', axis=0, tiled=True)  89.1 us
    ppermute x15, waiting for transfers between devices, partner_2(): return lax.ppermute(value, axis, pairs)  51.8 us
    ppermute x15, starting transfers between devices, partner_2(): return lax.ppermute(value, axis, pairs)  44.8 us
  transfers between devices with their start and end apart: 21, of which 21 were waited for; matrix products, arithmetic and copies ran while one was open for 1% of the time, Pallas kernels for 0%

profile of v1, /device:TPU:2, one launch (start us, length us, event | category | flops | bytes accessed | tf_op | source)
XLA Modules:
  0.0 981.1 jit_solution(546427932062317067)
XLA Ops:
  11.2 92.3 %all-gather.6.cloned.1.call-done = f32[32,8,2,64,128]{4,3,2,1,0:T(8,128)} async-done(((f32[1,8,2,64,128]{4,3,2,1,0:T(8,128)}), f32[32,8,2,64,128]{4,3,2,1,0:T(8,128)}) %all-gather.6.cloned.1.call-update) | async-done | bytes 16777232 | tf_op jit(solution)/shard_map/all_gather | solution.py:10
  103.4 7.5 reduce_sum.38
  111.7 33.5 %all_gather.37 = f32[1024,128]{1,0:T(8,128)S(1)} all-gather(f32[64,128]{1,0:T(8,128)S(1)} %fusion.30), channel_id=1, replica_groups=mesh['leaf'=32,'front'=16] {'front'}, dimensions={0}, use_global_device_ids=true | all-gather | bytes 557056 | tf_op jit(solution)/shard_map/all_gather | solution.py:65
  152.5 29.7 %all_gather.38 = f32[1024,128]{1,0:T(8,128)S(1)} all-gather(f32[64,128]{1,0:T(8,128)S(1)} %collective-permute-done), channel_id=1, replica_groups=mesh['leaf'=32,'front'=16] {'front'}, dimensions={0}, use_global_device_ids=true | all-gather | bytes 557056 | tf_op jit(solution)/shard_map/all_gather | solution.py:66
  184.6 64.6 %all-gather.8.cloned.1.call-done = f32[32,4,2,64,128]{4,3,2,1,0:T(8,128)} async-done(((f32[1,4,2,64,128]{4,3,2,1,0:T(8,128)}), f32[32,4,2,64,128]{4,3,2,1,0:T(8,128)}) %all-gather.8.cloned.1.call-update) | async-done | bytes 8388624 | tf_op jit(solution)/shard_map/all_gather | solution.py:10
  249.2 4.0 reduce_sum.39
  253.2 33.5 %all_gather.40 = f32[1024,128]{1,0:T(8,128)S(1)} all-gather(f32[64,128]{1,0:T(8,128)S(1)} %fusion.29), channel_id=1, replica_groups=mesh['leaf'=32,'front'=16] {'front'}, dimensions={0}, use_global_device_ids=true | all-gather | bytes 557056 | tf_op jit(solution)/shard_map/all_gather | solution.py:65
  292.6 29.7 %all_gather.41 = f32[1024,128]{1,0:T(8,128)S(1)} all-gather(f32[64,128]{1,0:T(8,128)S(1)} %collective-permute-done.1), channel_id=1, replica_groups=mesh['leaf'=32,'front'=16] {'front'}, dimensions={0}, use_global_device_ids=true | all-gather | bytes 557056 | tf_op jit(solution)/shard_map/all_gather | solution.py:66
  324.6 57.5 %all-gather.10.cloned.1.call-done = f32[32,2,2,64,128]{4,3,2,1,0:T(8,128)} async-done(((f32[1,2,2,64,128]{4,3,2,1,0:T(8,128)}), f32[32,2,2,64,128]{4,3,2,1,0:T(8,128)}) %all-gather.10.cloned.1.call-update) | async-done | bytes 4194320 | tf_op jit(solution)/shard_map/all_gather | solution.py:10
  384.5 33.5 %all_gather.43 = f32[1024,128]{1,0:T(8,128)S(1)} all-gather(f32[64,128]{1,0:T(8,128)S(1)} %fusion.28), channel_id=1, replica_groups=mesh['leaf'=32,'front'=16] {'front'}, dimensions={0}, use_global_device_ids=true | all-gather | bytes 557056 | tf_op jit(solution)/shard_map/all_gather | solution.py:65
  425.4 29.7 %all_gather.44 = f32[1024,128]{1,0:T(8,128)S(1)} all-gather(f32[64,128]{1,0:T(8,128)S(1)} %collective-permute-done.2), channel_id=1, replica_groups=mesh['leaf'=32,'front'=16] {'front'}, dimensions={0}, use_global_device_ids=true | all-gather | bytes 557056 | tf_op jit(solution)/shard_map/all_gather | solution.py:66
  457.3 55.4 %all-gather.12.cloned.1.call-done = f32[64,64,128]{2,1,0:T(8,128)} async-done(((f32[2,64,128]{2,1,0:T(8,128)}), f32[64,64,128]{2,1,0:T(8,128)}) %all-gather.12.cloned.1.call-update) | async-done | bytes 2097168 | tf_op jit(solution)/shard_map/all_gather | solution.py:10
  514.6 56.8 %psum.28 = f32[32,128]{1,0:T(8,128)S(1)} all-reduce(f32[32,128]{1,0:T(8,128)S(1)} %convolution_bitcast_fusion.5), channel_id=1, replica_groups=mesh['leaf'=32,'front'=16] {'front'}, use_global_device_ids=true, to_apply=%region_4.5 | all-reduce | flops 4096 | bytes 32768 | tf_op jit(solution)/shard_map/psum | solution.py:131
  583.7 4.3 collective-permute-done.5
  594.9 4.2 collective-permute-start.7
  599.1 5.6 collective-permute-done.7
  606.2 53.5 %psum.29 = f32[64,128]{1,0:T(8,128)S(1)} all-reduce(f32[64,128]{1,0:T(8,128)S(1)} %convolution_bitcast_fusion.4), channel_id=1, replica_groups=mesh['leaf'=32,'front'=16] {'front'}, use_global_device_ids=true, to_apply=%region_5.6 | all-reduce | flops 8192 | bytes 65536 | tf_op jit(solution)/shard_map/psum | solution.py:131
  665.0 4.0 collective-permute-done.9
  672.4 5.0 collective-permute-done.10
  680.5 5.2 collective-permute-done.11
  688.0 129.0 %all-reduce.3.cloned.1.call-done = f32[128,128]{0,1:T(8,128)} async-done(((f32[128,128]{0,1:T(8,128)}), f32[128,128]{0,1:T(8,128)}) %all-reduce.3.cloned.1.call-update) | async-done | bytes 65552 | tf_op jit(solution)/shard_map/psum | solution.py:131
  828.8 4.9 collective-permute-start.14
  835.3 4.4 collective-permute-done.14
  843.8 128.9 %all-reduce.5.cloned.1.call-done = f32[256,128]{0,1:T(8,128)} async-done(((f32[256,128]{0,1:T(8,128)}), f32[256,128]{0,1:T(8,128)}) %all-reduce.5.cloned.1.call-update) | async-done | bytes 131088 | tf_op jit(solution)/shard_map/psum | solution.py:131
  (127 shorter events, 89.8 us)
Async XLA Ops:
  7.2 96.2 %all-gather.6.cloned.1.call-start = ((), (), s32[]{:S(2)}) async-start(), calls=%async_computation | async-start | bytes 17301504 | tf_op jit(solution)/shard_map/all_gather | solution.py:10
  10.2 239.0 %all-gather.8.cloned.1.call-start = ((), (), s32[]{:S(2)}) async-start(), calls=%async_computation.1 | async-start | bytes 8650752 | tf_op jit(solution)/shard_map/all_gather | solution.py:10
  11.2 172.3 %copy-start.3 = (f32[2,64,128]{2,1,0:T(8,128)S(1)}, f32[2,64,128]{2,1,0:T(8,128)}, u32[]{:S(2)}) copy-start(f32[2,64,128]{2,1,0:T(8,128)} %param.13) | copy-start | bytes 196612
  11.2 172.3 %copy-start.6 = (f32[128,128]{1,0:T(8,128)S(1)}, f32[128,128]{1,0:T(8,128)}, u32[]{:S(2)}) copy-start(f32[128,128]{1,0:T(8,128)} %param.17) | copy-start | bytes 196612
  145.2 7.3 collective-permute-start
  183.6 139.8 %copy-start.2 = (f32[2,64,64]{2,1,0:T(8,128)S(1)}, f32[2,64,64]{2,1,0:T(8,128)}, u32[]{:S(2)}) copy-start(f32[2,64,64]{2,1,0:T(8,128)} %param.12) | copy-start | bytes 98308
  184.5 197.6 %all-gather.10.cloned.1.call-start = ((), (), s32[]{:S(2)}) async-start(), calls=%async_computation.2 | async-start | bytes 4325376 | tf_op jit(solution)/shard_map/all_gather | solution.py:10
  286.8 5.8 collective-permute-start.1
  324.5 188.2 %all-gather.12.cloned.1.call-start = ((), (), s32[]{:S(2)}) async-start(), calls=%async_computation.5 | async-start | bytes 2162688 | tf_op jit(solution)/shard_map/all_gather | solution.py:10
  418.1 7.3 collective-permute-start.2
  457.3 359.7 %all-reduce.3.cloned.1.call-start = ((), (), s32[]{:S(2)}) async-start(), calls=%async_computation.3 | async-start | bytes 131072 | tf_op jit(solution)/shard_map/psum | solution.py:131
  571.4 3.1 collective-permute-start.3
  574.5 5.8 collective-permute-start.4
  580.3 7.7 collective-permute-start.5
  588.0 6.9 collective-permute-start.6
  594.9 9.8 collective-permute-start.7
  659.7 3.1 collective-permute-start.8
  662.8 6.2 collective-permute-start.9
  669.0 8.4 collective-permute-start.10
  677.4 8.3 collective-permute-start.11
  687.9 284.8 %all-reduce.5.cloned.1.call-start = ((), (), s32[]{:S(2)}) async-start(), calls=%async_computation.4 | async-start | bytes 262144 | tf_op jit(solution)/shard_map/psum | solution.py:131
  816.9 3.5 collective-permute-start.12
  821.4 7.5 collective-permute-start.13
  828.8 10.9 %collective-permute-start.14 = (f32[512,128]{0,1:T(8,128)S(1)}, f32[512,128]{0,1:T(8,128)S(1)}, u32[]{:S(2)}, u32[]{:S(2)}) collective-permute-start(f32[512,128]{0,1:T(8,128)S(1)} %maximum_select_fusion.5), channel_id=1, source_target_pairs={{0,64},{16,80},{32,96},{48,112},{64,0},{80,16},{96,32},{112,48},{1... | collective-permute-start | bytes 786440 | tf_op jit(solution)/shard_map/ppermute | solution.py:17
  (6 other events, 569.9 us)
Sparse Core Ops, SparseCore 0:
  11.2 92.2 all-gather.5
  184.6 64.5 all-gather.7
  324.6 57.4 all-gather.9
  457.4 55.2 all-gather.11
  688.0 128.8 all-reduce.2
  842.6 130.0 all-reduce.4
